TPU v7x, 256 devices: a whole 4x4x8 slice. The times are simulated.
256 devices in a mesh: row: 16 (over z_hi, x, core), col: 16 (over z_lo, y).
Axes of the slice: x: 4, y: 4, z: 8 (z_hi: 2, z_lo: 4; z = z_hi * 4 + z_lo), core: 2. Of those that a mesh axis runs over, the one named last changes fastest.
Arguments:
- basis: bfloat16 [65536, 2048], P('row', 'col'), may hold values from -0.375 to 0.375
- stiffness: bfloat16 [2, 1024, 64, 512], P(None, 'row'), may hold values from -0.25 to 0.25
- block_cols: int32 [1024, 8], P('row'), may hold values from 0 to 1023, as said below
- block_counts: int32 [1024], P('row'), may hold values from 3 to 8
Outputs:
- reduced: float32 [2048, 2, 2048], P('row', None, 'col')
Inputs may be any that keep to these rules, and one draw needn't show every extreme that they name: `block_cols`: each entry lies within 2 of its block row's own index; slot 0 is the block row itself, slot 1 and slot 2 lie 2 before and after it (clipped to the mesh).
All inputs are finite; a program needn't handle non-finite values.
Results may differ from a plain program's by a relative error of at most 0.0029.
Values may be sent and summed in bfloat16 or wider, within the bound.
A program may use at most 128 MiB of HBM per device.

v0:
```python
import jax
import jax.numpy as jnp
from jax import lax
from jax.sharding import PartitionSpec as P

BLOCK = 64
CAP = 8
HB = 2


def extended(block, sides, width):
    for axis, dim in sides:
        count = lax.axis_size(axis)
        forward = [(i, i + 1) for i in range(count - 1)]
        backward = [(target, source) for source, target in forward]
        low = lax.ppermute(
            lax.slice_in_dim(block, block.shape[dim] - width, None, axis=dim), axis, forward
        )
        high = lax.ppermute(lax.slice_in_dim(block, 0, width, axis=dim), axis, backward)
        block = jnp.concatenate([low, block, high], axis=dim)
    return block


def shards(basis, stiffness, block_cols, block_counts):
    rows_dev, panel = basis.shape
    blocks_dev = rows_dev // BLOCK
    padded = extended(basis, (("row", 0),), HB * BLOCK)
    framed = padded.reshape(blocks_dev + 2 * HB, BLOCK, panel)
    first = lax.axis_index("row") * blocks_dev - HB
    local_cols = block_cols - first
    slots = jnp.arange(CAP, dtype=jnp.int32)
    live = (slots[None, :] < block_counts[:, None]).astype(jnp.bfloat16)
    picked = framed[local_cols] * live[:, :, None, None]
    picked = picked.reshape(blocks_dev, CAP * BLOCK, panel)
    applied = jnp.einsum("qnrk,nkp->qnrp", stiffness, picked, preferred_element_type=jnp.float32)
    applied = applied.astype(jnp.bfloat16).reshape(2, rows_dev, panel)
    stacked = jnp.concatenate([applied[0], applied[1]], axis=1)
    last_row = (lax.axis_index("col") + 1) * panel
    share = panel * lax.axis_size("col") // lax.axis_size("row")
    piece = lax.all_gather(basis, "col", axis=1, tiled=True)
    count = piece.shape[1]
    partial_value = lax.dot_general(
        piece, stacked, (((0,), (0,)), ((), ())), preferred_element_type=jnp.float32
    )
    index = jnp.arange(count, dtype=jnp.int32)
    term = jnp.where((index < last_row)[:, None], partial_value, 0.0)
    mine = lax.psum_scatter(term, "row", scatter_dimension=0, tiled=True)
    return mine.reshape(share, 2, panel)


def solution(mesh):
    return jax.shard_map(
        shards,
        mesh=mesh,
        in_specs=(P("row", "col"), P(None, "row", None, None), P("row", None), P("row")),
        out_specs=P("row", None, "col"),
        check_vma=False,
    )
```

profile of v0, /device:TPU:97, one launch (start us, length us, event | category | flops | bytes accessed | tf_op | source)
XLA Modules:
  0.0 314.5 jit_solution(8450057766222515610)
XLA Ops:
  6.5 0.0 all-gather.2.cloned.1.call-start
  6.5 0.7 all-gather.2.cloned.1.call-update
  7.3 0.0 reduce-scatter.2.cloned.1.call-start
  7.3 0.8 fusion.14
  8.1 3.7 %collective-permute-start = (bf16[128,128]{1,0:T(8,128)(2,1)S(1)}, bf16[128,128]{1,0:T(8,128)(2,1)S(1)}, u32[]{:S(2)}, u32[]{:S(2)}) collective-permute-start(bf16[128,128]{1,0:T(8,128)(2,1)S(1)} %get-tuple-element.7), channel_id=1, source_target_pairs={{0,16},{16,32},{32,48},{48,64},{64,80},{80,96},{96,112},{112,128},... | collective-permute-start | bytes 98312 | tf_op jit(solution)/shard_map/ppermute | solution.py:16
  11.8 1.9 collective-permute-start.1
  13.7 0.7 compare_select_fusion
  14.4 0.1 copy.7
  14.5 0.1 reshape.44
  14.6 0.7 fusion.11
  15.3 0.1 mul.21
  15.5 0.1 mul.22
  15.6 0.0 collective-permute-done
  15.6 1.4 collective-permute-done.1
  17.0 1.3 pad_maximum_fusion
  18.3 13.5 %gather_fusion = bf16[512,64,128]{2,1,0:T(8,128)(2,1)} fusion(bf16[68,64,128]{2,1,0:T(8,128)(2,1)S(1)} %bitcast.19, s32[1024]{0:T(1024)S(1)} %pad_clamp_fusion), kind=kCustom, calls=%fused_computation | custom fusion | bytes 16779264 | tf_op jit(solution)/shard_map/gather | solution.py:33
  31.8 8.6 %bitcast_multiply_fusion = bf16[64,512,128]{2,1,0:T(8,128)(2,1)} fusion(bf16[64,512]{1,0:T(8,128)(2,1)S(1)} %mul.22, bf16[64,512,128]{2,1,0:T(8,128)(2,1)} %bitcast.20), kind=kLoop, calls=%fused_computation.3 | loop fusion | flops 4194304 | bytes 16842752 | tf_op jit(solution)/shard_map/mul | solution.py:33
  40.4 7.4 %convert_bitcast_fusion = bf16[2,64,64,128]{3,2,0,1:T(8,128)(2,1)S(1)} fusion(bf16[2,64,64,512]{3,2,1,0:T(8,128)(2,1)} %param.5, bf16[64,512,128]{2,1,0:T(8,128)(2,1)} %bitcast_multiply_fusion), kind=kOutput, calls=%fused_computation.10 | convolution fusion | flops 1074790400 | bytes 18874368 | tf_op jit(solution)/shard_map/qnrk,nkp->qnrp/dot_general | solution.py:35
  47.8 1.2 fusion.13
  49.0 153.0 %all-gather.2.cloned.1.call-done = bf16[4096,2048]{1,0:T(8,128)(2,1)} async-done(((bf16[4096,128]{1,0:T(8,128)(2,1)}), bf16[4096,2048]{1,0:T(8,128)(2,1)}) %all-gather.2.cloned.1.call-update) | async-done | bytes 16777232 | tf_op jit(solution)/shard_map/all_gather | solution.py:40
  202.0 12.0 %fusion.3 = f32[2048,256]{0,1:T(8,128)} fusion(bf16[4096,2048]{1,0:T(8,128)(2,1)} %all-gather.2.cloned.1.call-done, bf16[4096,128]{1,0:T(8,128)(2,1)} %bitcast.22, bf16[4096,128]{1,0:T(8,128)(2,1)S(1)} %bitcast.21, pred[2048]{0:T(1024)(128)(4,1)S(1)} %iota_compare_fusion.1), kind=kOutput, calls=%fused_computation.6 | convolution fusion | flops 4299685888 | bytes 20973568 | tf_op jit(solution)/shard_map/dot_general | solution.py:42
  214.0 0.0 reduce-scatter.2.cloned.1.call-update
  214.0 92.0 %reduce-scatter.2.cloned.1.call-done = f32[128,256]{0,1:T(8,128)} async-done(((f32[2048,256]{0,1:T(8,128)}), f32[128,256]{0,1:T(8,128)}) %reduce-scatter.2.cloned.1.call-update) | async-done | bytes 131088 | tf_op jit(solution)/shard_map/reduce_scatter | solution.py:47
  306.0 1.7 copy.9
  (2 shorter events, 0.0 us)
Async XLA Ops:
  6.5 195.4 %all-gather.2.cloned.1.call-start = ((), (), s32[]{:S(2)}) async-start(), calls=%async_computation.1 | async-start | bytes 17825792 | tf_op jit(solution)/shard_map/all_gather | solution.py:40
  7.3 298.7 %reduce-scatter.2.cloned.1.call-start = ((), (), s32[]{:S(2)}) async-start(), calls=%async_computation.2 | async-start | bytes 2228224 | tf_op jit(solution)/shard_map/reduce_scatter | solution.py:47
  8.1 7.5 %collective-permute-start = (bf16[128,128]{1,0:T(8,128)(2,1)S(1)}, bf16[128,128]{1,0:T(8,128)(2,1)S(1)}, u32[]{:S(2)}, u32[]{:S(2)}) collective-permute-start(bf16[128,128]{1,0:T(8,128)(2,1)S(1)} %get-tuple-element.7), channel_id=1, source_target_pairs={{0,16},{16,32},{32,48},{48,64},{64,80},{80,96},{96,112},{112,128},... | collective-permute-start | bytes 98312 | tf_op jit(solution)/shard_map/ppermute | solution.py:16
  11.8 5.2 %collective-permute-start.1 = (bf16[128,128]{1,0:T(8,128)(2,1)S(1)}, bf16[128,128]{1,0:T(8,128)(2,1)S(1)}, u32[]{:S(2)}, u32[]{:S(2)}) collective-permute-start(bf16[128,128]{1,0:T(8,128)(2,1)S(1)} %get-tuple-element.8), channel_id=1, source_target_pairs={{16,0},{32,16},{48,32},{64,48},{80,64},{96,80},{112,96},{128,112},... | collective-permute-start | bytes 98312 | tf_op jit(solution)/shard_map/ppermute | solution.py:19
Sparse Core Ops, SparseCore 0:
  9.1 192.8 all-gather.1
  214.1 91.7 reduce-scatter.1
where the time goes:
time: 320 us; the launch traced here: 314 us
  waiting for transfers between devices  247 us (77%)
  matrix products  19.5 us (6%)
  local copies, waits for them, and re-layouts  17.6 us (6%)
  between operations  13.5 us (4%)
  other arithmetic  11.3 us (4%)
  starting transfers between devices  5.63 us (2%)
    all_gather x1, waiting for transfers between devices, shards(): piece = lax.all_gather(basis, 'col', axis=1, tiled=True)  153 us
    reduce_scatter x1, waiting for transfers between devices, shards(): mine = lax.psum_scatter(term, 'row', scatter_dimension=0, tiled=True)  92 us
    gather x1, local copies, waits for them, and re-layouts, shards(): picked = framed[local_cols] * live[:, :, None, None]  13.5 us
    dot_general x1, matrix products, shards(): lax.dot_general(piece, stacked, (((0,), (0,)), ((), ())), preferred_eleme...  12 us
    mul x1, other arithmetic, shards(): picked = framed[local_cols] * live[:, :, None, None]  8.59 us
    dot_general x1, matrix products, shards(): jnp.einsum('qnrk,nkp->qnrp', stiffness, picked, preferred_element_type=jn...  7.45 us
  transfers between devices with their start and end apart: 4, of which 3 were waited for; matrix products, arithmetic and copies ran while one was open for 11% of the time, Pallas kernels for 0%

commit v1 on v0

v1 whole, which is shorter than its diff:
```python
import jax
import jax.numpy as jnp
from jax import lax
from jax.experimental import pallas as pl
from jax.experimental.pallas import tpu as pltpu
from jax.sharding import PartitionSpec as P

MESH = pl.DeviceIdType.MESH
BF = jnp.bfloat16
F32 = jnp.float32
BLOCK = 64
CAP = 8
HALO = 2 * BLOCK
ROWS = 4096
HALF = ROWS // 2
NB = HALF // BLOCK
EXT = HALF + 2 * HALO
DEAD = EXT // BLOCK
PAN = 128


def kernel(idx, basis_ref, stiff_ref, out_ref,
           sv, ox, ya, yh, zu, zd, g, pt, zt, ap, az, acc, r1, s2, r2, fin,
           lsem, hs, hr, fs, fr, ys, yr, zus, zur, zds, zdr, s1s, s1r, s2s, s2r, s3s, s3r):
    r = lax.axis_index("row")
    c = lax.axis_index("col")
    core, x, zh = r % 2, (r // 2) % 4, r // 8
    a, b = c // 4, c % 4

    load_own = pltpu.make_async_copy(basis_ref, ox.at[pl.ds(HALO, ROWS)], lsem.at[0])
    load_own.start()
    load_s = pltpu.make_async_copy(stiff_ref, sv, lsem.at[1])
    load_s.start()

    def yb(d):
        return (b + d) % 4

    def ycol(d):
        return a * 4 + yb(d)

    def zcol(z):
        return z * 4 + b

    up_row, down_row = (r + 1) % 16, (r + 15) % 16
    barrier = pltpu.get_barrier_semaphore()
    other_zh = (1 - zh) * 8 + x * 2 + core
    partners = [(up_row, c), (down_row, c), (other_zh, c)]
    partners += [(zh * 8 + ((x + d) % 4) * 2 + core, c) for d in (1, 2, 3)]
    for d in (1, 2, 3):
        for row in (r, other_zh):
            partners += [(row, ycol(d)), (row, zcol((a + d) % 4))]
    for dev in partners:
        pl.semaphore_signal(barrier, inc=1, device_id=dev, device_id_type=MESH)
    pl.semaphore_wait(barrier, len(partners))

    def remote(src, dst, ss, rs, dev):
        return pltpu.make_async_remote_copy(src_ref=src, dst_ref=dst, send_sem=ss, recv_sem=rs,
                                            device_id=dev, device_id_type=MESH)

    halo_up = remote(ox.at[pl.ds(ROWS, HALO)], ox.at[pl.ds(0, HALO)], hs.at[0], hr.at[0], (up_row, c))
    halo_down = remote(ox.at[pl.ds(HALO, HALO)], ox.at[pl.ds(ROWS + HALO, HALO)], hs.at[1], hr.at[1], (down_row, c))
    own_lo = ox.at[pl.ds(HALO, HALF)]
    own_hi = ox.at[pl.ds(HALO + HALF, HALF)]
    nxt, prv = (r, ycol(1)), (r, ycol(3))
    y_lo_n = remote(own_lo, ya.at[1, pl.ds(HALO, HALF)], ys.at[0], yr.at[0], nxt)
    y_hi_n = remote(own_hi, yh.at[1], ys.at[1], yr.at[1], nxt)
    y_hi_p = remote(own_hi, yh.at[0], ys.at[2], yr.at[2], prv)
    y_lo_p = remote(own_lo, ya.at[0, pl.ds(HALO, HALF)], ys.at[3], yr.at[3], prv)
    y_lo_f = remote(ya.at[1, pl.ds(HALO, HALF)], ya.at[2, pl.ds(HALO, HALF)], ys.at[4], yr.at[4], nxt)
    y_hi_f = remote(yh.at[0], yh.at[2], ys.at[5], yr.at[5], prv)

    zup = (r, zcol((a + 1) % 4))
    zdn = (r, zcol((a + 3) % 4))
    DN = HALF + HALO
    zu_cp = [remote(own_lo, zu.at[0], zus.at[0], zur.at[0], zup)]
    zd_cp = [remote(ox.at[pl.ds(HALF, DN)], zd.at[0, pl.ds(0, DN)], zds.at[0], zdr.at[0], zdn)]
    for d in (1, 2):
        zu_cp.append(remote(zu.at[d - 1], zu.at[d], zus.at[d], zur.at[d], zup))
        zd_cp.append(remote(zd.at[d - 1, pl.ds(0, DN)], zd.at[d, pl.ds(0, DN)], zds.at[d], zdr.at[d], zdn))

    load_own.wait()
    halo_up.start()
    halo_down.start()

    @pl.when(a < 3)
    def _():
        zu_cp[0].start()

    @pl.when(a > 0)
    def _():
        zd_cp[0].start()

    y_lo_n.start()
    y_hi_p.start()
    y_hi_n.start()
    y_lo_p.start()

    g[DEAD] = jnp.zeros((BLOCK, 2 * PAN), BF)

    halo_up.wait_recv()
    halo_down.wait_recv()
    fan_lo = [remote(ox.at[pl.ds(0, HALO)], ya.at[s - 1, pl.ds(0, HALO)], fs.at[s - 1], fr.at[s - 1], (r, ycol(dy)))
              for s, dy in ((1, 3), (2, 1), (3, 2))]
    fan_hi = [remote(ox.at[pl.ds(HALO + ROWS, HALO)], zd.at[d - 1, pl.ds(DN, HALO)], fs.at[2 + d], fr.at[2 + d],
                     (r, zcol((a + 4 - d) % 4))) for d in (1, 2, 3)]
    for cp in fan_lo:
        cp.start()
    for d in (1, 2, 3):
        @pl.when(a >= d)
        def _():
            fan_hi[d - 1].start()

    def apply(h, outs):
        n = len(outs) * PAN

        def step(i, carry):
            row = h * NB + i
            lhs = jnp.concatenate([sv[0, row], sv[1, row]], axis=0)
            picked = jnp.concatenate(
                [g[idx[row * CAP + s]][:, 0:n] for s in range(CAP)], axis=0)
            res = jnp.dot(lhs, picked, preferred_element_type=F32).astype(BF)
            at = pl.ds(pl.multiple_of(i * BLOCK, BLOCK), BLOCK)
            for p, (ref, k) in enumerate(outs):
                for q in range(2):
                    ref[k, at, q * PAN:(q + 1) * PAN] = res[q * BLOCK:(q + 1) * BLOCK, p * PAN:(p + 1) * PAN]
            return carry

        lax.fori_loop(0, NB, step, 0, unroll=2)

    def put(rows, at, lane):
        n = rows.shape[0] // BLOCK
        g[at:at + n, :, lane:lane + PAN] = rows.reshape(n, BLOCK, PAN)

    def take_y(s, lane):
        put(ya[s - 1], 0, lane)
        put(yh[s - 1, 0:HALO], DEAD - 2, lane)

    def turn_y(s):
        pt[0, s * PAN:(s + 1) * PAN, :] = ya[s - 1, HALO:HALO + HALF, :].T
        pt[1, s * PAN:(s + 1) * PAN, :] = yh[s - 1].T

    def down(d, lo, hi):
        res = jnp.dot(pt[1, lo * PAN:hi * PAN, :], az[d], preferred_element_type=F32)
        if d == 0:
            res += jnp.dot(pt[0, lo * PAN:hi * PAN, :], ap[0], preferred_element_type=F32)
        acc[a + d, lo * PAN:hi * PAN, :] = res

    def up(d, s):
        acc[a - d, s * PAN:(s + 1) * PAN, :] = jnp.dot(zt[d - 1], ap[s], preferred_element_type=F32)

    load_s.wait()
    put(ox[0:EXT, :], 0, 0)
    apply(0, [(ap, 0)])
    pt[0, 0:PAN, :] = ox[HALO:HALO + HALF, :].T
    pt[1, 0:PAN, :] = ox[HALO + HALF:HALO + ROWS, :].T

    @pl.when(a > 0)
    def _():
        zu_cp[0].wait_recv()

    @pl.when((a > 0) & (a < 3))
    def _():
        zu_cp[1].start()

    @pl.when(a < 3)
    def _():
        zd_cp[0].wait_recv()

    @pl.when((a < 3) & (a > 0))
    def _():
        zd_cp[1].start()

    y_lo_n.wait_recv()
    y_lo_f.start()
    y_hi_p.wait_recv()
    y_hi_f.start()

    put(ox[HALF:HALF + EXT, :], 0, 0)

    @pl.when(a < 3)
    def _():
        fan_hi[0].wait_recv()
        put(zd[0], 0, PAN)
        apply(1, [(az, 0), (az, 1)])

    @pl.when(a == 3)
    def _():
        apply(1, [(az, 0)])

    @pl.when(a > 1)
    def _():
        zu_cp[1].wait_recv()

    @pl.when(a == 2)
    def _():
        zu_cp[2].start()

    @pl.when(a < 2)
    def _():
        zd_cp[1].wait_recv()

    @pl.when(a == 1)
    def _():
        zd_cp[2].start()

    y_hi_n.wait_recv()
    y_lo_p.wait_recv()
    for s in (1, 2):
        fan_lo[s - 1].wait_recv()
        turn_y(s)

    @pl.when(a > 0)
    def _():
        take_y(1, 0)
        take_y(2, PAN)
        apply(0, [(ap, 1), (ap, 2)])
        zt[0] = zu[0].T
        for s in (0, 1, 2):
            up(1, s)

    @pl.when(a > 1)
    def _():
        zt[1] = zu[1].T
        for s in (0, 1, 2):
            up(2, s)

    down(0, 0, 3)

    @pl.when(a < 3)
    def _():
        down(1, 0, 3)

    @pl.when(a < 2)
    def _():
        fan_hi[1].wait_recv()
        put(zd[1], 0, 0)
        apply(1, [(az, 2)])
        down(2, 0, 3)

    def block(k):
        z, s = k // 4, k % 4
        y = (b + s + (s // 2) * (1 - 2 * (s % 2))) % 4
        left = jnp.where(z < a, z * 4 + b, a * 4 + y)
        right = jnp.where(z < a, a * 4 + y, z * 4 + b)
        used = (z != a) | (y <= b)
        early = (s != 3) & (z - a != 3) & (a - z != 3)
        return z, s, left, right, used, early

    def at(k):
        return acc.at[k // 4, pl.ds(pl.multiple_of((k % 4) * PAN, PAN), PAN), :]

    def pair_copy(k):
        return remote(at(k), r1.at[k], s1s.at[k], s1r.at[k], (zh * 8 + x * 2 + (1 - core), c))

    def x_copy(k, xp):
        place = (x - xp + 4) % 4 - 1
        return remote(s2.at[k], r2.at[k, place], s2s.at[k], s2r.at[k, place], (zh * 8 + xp * 2 + core, c))

    def last_copy(k, z, left, right):
        place = jnp.where(z < a, 0, 2) + zh
        return remote(at(k), fin.at[place], s3s.at[k], s3r.at[place], (left, right))

    def loop(fn):
        def step(k, carry):
            fn(k)
            return carry
        lax.fori_loop(0, 16, step, 0)

    def pair_send(late):
        def fn(k):
            z, s, left, right, used, early = block(k)

            @pl.when(used & (early != late) & (left % 2 != core))
            def _():
                pair_copy(k).start()
        loop(fn)

    def pair_sum(late):
        def fn(k):
            z, s, left, right, used, early = block(k)
            xp = (left // 2) % 4

            @pl.when(used & (early != late) & (left % 2 == core))
            def _():
                pair_copy(k).wait_recv()
                total = at(k)[...] + r1[k]

                @pl.when(xp == x)
                def _():
                    at(k)[...] = total

                @pl.when(xp != x)
                def _():
                    s2[k] = total.astype(BF)
                    x_copy(k, xp).start()
        loop(fn)

    def x_sum():
        def fn(k):
            z, s, left, right, used, early = block(k)
            xp = (left // 2) % 4

            @pl.when(used & (left % 2 == core) & (xp == x))
            def _():
                total = at(k)[...]
                for place in range(3):
                    remote(s2.at[k], r2.at[k, place], s2s.at[k], s2r.at[k, place], (r, c)).wait_recv()
                    total += r2[k, place].astype(F32)
                self = (left == r) & (right == c)

                @pl.when(self)
                def _():
                    fin[jnp.where(z < a, 0, 2) + zh] = total

                @pl.when(jnp.logical_not(self))
                def _():
                    at(k)[...] = total
                    last_copy(k, z, left, right).start()
        loop(fn)

    pair_send(False)
    pair_sum(False)

    y_lo_f.wait_recv()
    y_hi_f.wait_recv()
    fan_lo[2].wait_recv()
    turn_y(3)

    @pl.when(a == 3)
    def _():
        zu_cp[2].wait_recv()
        zt[2] = zu[2].T
        for s in (0, 1, 2):
            up(3, s)

    @pl.when(a == 0)
    def _():
        zd_cp[2].wait_recv()
        fan_hi[2].wait_recv()
        put(zd[2], 0, 0)
        apply(1, [(az, 3)])
        down(3, 0, 4)

    @pl.when(a > 0)
    def _():
        take_y(3, 0)
        apply(0, [(ap, 3)])

    for d in (1, 2, 3):
        @pl.when(a >= d)
        def _():
            up(d, 3)

    down(0, 3, 4)
    for d in (1, 2):
        @pl.when(a + d < 4)
        def _():
            down(d, 3, 4)

    pair_send(True)
    pair_sum(True)
    x_sum()

    zi, yi = r // 4, r % 4
    cross = zi < a
    plane = (zi == a) & (yi <= b)

    def fin_wait(place):
        remote(fin.at[place], fin.at[place], s3s.at[0], s3r.at[place], (r, c)).wait_recv()

    for place in range(4):
        if place < 2:
            needed = cross & jnp.logical_not((yi == b) & (zh == place))
        else:
            needed = cross | (plane & (zh != place - 2))

        @pl.when(needed)
        def _():
            fin_wait(place)

    @pl.when(cross)
    def _():
        out_ref[...] = (fin[0] + fin[1]) + (fin[2] + fin[3])

    @pl.when(plane)
    def _():
        out_ref[...] = fin[2] + fin[3]

    @pl.when(jnp.logical_not(cross | plane))
    def _():
        out_ref[...] = jnp.zeros_like(out_ref)

    for cp in [halo_up, halo_down, y_lo_n, y_hi_n, y_hi_p, y_lo_p, y_lo_f, y_hi_f] + fan_lo:
        cp.wait_send()
    for d in (1, 2, 3):
        @pl.when(a >= d)
        def _():
            fan_hi[d - 1].wait_send()

        @pl.when((a >= d - 1) & (a < 3))
        def _():
            zu_cp[d - 1].wait_send()

        @pl.when((a + d - 1 <= 3) & (a > 0))
        def _():
            zd_cp[d - 1].wait_send()

    def drain(k):
        z, s, left, right, used, early = block(k)
        xp = (left // 2) % 4

        @pl.when(used & (left % 2 != core))
        def _():
            pair_copy(k).wait_send()

        @pl.when(used & (left % 2 == core) & (xp != x))
        def _():
            x_copy(k, xp).wait_send()

        @pl.when(used & (left % 2 == core) & (xp == x) & jnp.logical_not((left == r) & (right == c)))
        def _():
            last_copy(k, z, left, right).wait_send()

    loop(drain)


def shards(basis, stiffness, block_cols, block_counts):
    dma = pltpu.SemaphoreType.DMA
    rows = jnp.arange(2 * NB, dtype=jnp.int32)
    first = lax.axis_index("row") * (2 * NB) - 2 + (rows // NB) * NB
    live = jnp.arange(CAP, dtype=jnp.int32)[None, :] < block_counts[:, None]
    idx = jnp.where(live, block_cols - first[:, None], DEAD)
    out = pl.pallas_call(
        kernel,
        out_shape=jax.ShapeDtypeStruct((PAN, 2 * PAN), F32),
        in_specs=[
            pl.BlockSpec(memory_space=pltpu.SMEM),
            pl.BlockSpec(memory_space=pltpu.HBM),
            pl.BlockSpec(memory_space=pltpu.HBM),
        ],
        out_specs=pl.BlockSpec(memory_space=pltpu.VMEM),
        scratch_shapes=[
            pltpu.VMEM((2, 2 * NB, BLOCK, CAP * BLOCK), BF),
            pltpu.VMEM((ROWS + 2 * HALO, PAN), BF),
            pltpu.VMEM((3, HALO + HALF, PAN), BF),
            pltpu.VMEM((3, HALF, PAN), BF),
            pltpu.VMEM((3, HALF, PAN), BF),
            pltpu.VMEM((3, EXT, PAN), BF),
            pltpu.VMEM((DEAD + 1, BLOCK, 2 * PAN), BF),
            pltpu.VMEM((2, 4 * PAN, HALF), BF),
            pltpu.VMEM((3, PAN, HALF), BF),
            pltpu.VMEM((4, HALF, 2 * PAN), BF),
            pltpu.VMEM((4, HALF, 2 * PAN), BF),
            pltpu.VMEM((4, 4 * PAN, 2 * PAN), F32),
            pltpu.VMEM((16, PAN, 2 * PAN), F32),
            pltpu.VMEM((16, PAN, 2 * PAN), BF),
            pltpu.VMEM((16, 3, PAN, 2 * PAN), BF),
            pltpu.VMEM((4, PAN, 2 * PAN), F32),
            dma((2,)), dma((2,)), dma((2,)), dma((6,)), dma((6,)), dma((6,)), dma((6,)),
            dma((3,)), dma((3,)), dma((3,)), dma((3,)),
            dma((16,)), dma((16,)), dma((16,)), dma((16, 3)), dma((16,)), dma((4,)),
        ],
        compiler_params=pltpu.CompilerParams(
            collective_id=0, has_side_effects=True, vmem_limit_bytes=56 * 2**20),
        cost_estimate=pl.CostEstimate(flops=8 * 10**9, bytes_accessed=10 * 2**20, transcendentals=0),
    )(idx.reshape(-1), basis, stiffness)
    return out.reshape(PAN, 2, PAN)


def solution(mesh):
    return jax.shard_map(
        shards,
        mesh=mesh,
        in_specs=(P("row", "col"), P(None, "row", None, None), P("row", None), P("row")),
        out_specs=P("row", None, "col"),
        check_vma=False,
    )
```

time: 320 us -> 84.1 us (0.26); the launches traced: 314 us -> 82.5 us
  waiting for transfers between devices: 247 us -> 0 us
  Pallas kernels: 0 us -> 79.4 us
  matrix products: 19.5 us -> 0 us
  local copies, waits for them, and re-layouts: 17.6 us -> 2.38 us
  between operations: 13.5 us -> 0.01 us
  other arithmetic: 11.3 us -> 0.7 us
  starting transfers between devices: 5.63 us -> 0 us
    all_gather x1 -> x0, waiting for transfers between devices: 153 us -> none  [shards(): piece = lax.all_gather(basis, 'col', axis=1, tiled=True)]
    reduce_scatter x1 -> x0, waiting for transfers between devices: 92 us -> none  [shards(): mine = lax.psum_scatter(term, 'row', scatter_dimension=0, tiled=True)]
    pallas_call x0 -> x1, Pallas kernels: none -> 79.4 us  [shards(): pl.pallas_call(kernel, out_shape=jax.ShapeDtypeStruct((PAN, 2 * PAN), F32...]
    dot_general x2 -> x0, matrix products: 19.5 us -> none  [the longest x1 12 us: shards(): lax.dot_general(piece, stacked, (((0,), (0,)), ((), ())), preferred_eleme...]
    gather x1 -> x0, local copies, waits for them, and re-layouts: 13.5 us -> none  [shards(): picked = framed[local_cols] * live[:, :, None, None]]
    mul x1 -> x0, other arithmetic: 8.59 us -> none  [shards(): picked = framed[local_cols] * live[:, :, None, None]]
    ppermute x2 -> x0, starting transfers between devices: 5.59 us -> none  [the longest x1 3.67 us: extended(): lax.ppermute(lax.slice_in_dim(block, block.shape[dim] - width, None, axis...]
  transfers between devices with their start and end apart: 4 -> 0, of which waited for: 3 -> 0; matrix products, arithmetic and copies ran while one was open for 11% -> 0% of each run, Pallas kernels for 0% -> 0%
where the time goes in v1:
time: 84.1 us; the launch traced here: 82.5 us
  Pallas kernels  79.4 us (94%)
  local copies, waits for them, and re-layouts  2.38 us (3%)
    pallas_call x1, Pallas kernels, shards(): pl.pallas_call(kernel, out_shape=jax.ShapeDtypeStruct((PAN, 2 * PAN), F32...  79.4 us

profile of v1, /device:TPU:97, one launch (start us, length us, event | category | flops | bytes accessed | tf_op | source)
XLA Modules:
  0.0 82.5 jit_solution(2310601860346286826)
XLA Ops:
  0.0 0.7 subtract_select_fusion
  0.7 0.1 copy.5
  0.8 0.7 reshape.22.idx
  1.5 79.4 %shard_map.46 = f32[128,256]{1,0:T(8,128)} custom-call(s32[512]{0:T(512)} %reshape.22.idx, bf16[4096,128]{1,0:T(8,128)(2,1)} %basis_ref.1, bf16[2,64,64,512]{3,2,1,0:T(8,128)(2,1)} %stiff_ref.1), custom_call_target="tpu_custom_call" | custom-call | flops 8000000000 | bytes 10485760 | tf_op jit(solution)/shard_map/pallas_call | solution.py:433
  80.9 1.6 %reshape.23 = f32[128,2,128]{2,1,0:T(2,128)} reshape(f32[128,256]{1,0:T(8,128)} %shard_map.46) | data formatting | bytes 262144 | tf_op jit(solution)/shard_map/reshape | solution.py:467
  (1 shorter events, 0.0 us)

commit v2 on v1

v2 whole, which is shorter than its diff:
```python
import jax
import jax.numpy as jnp
from jax import lax
from jax.experimental import pallas as pl
from jax.experimental.pallas import tpu as pltpu
from jax.sharding import PartitionSpec as P

MESH = pl.DeviceIdType.MESH
BF = jnp.bfloat16
F32 = jnp.float32
BLOCK = 64
CAP = 8
HALO = 2 * BLOCK
ROWS = 4096
HALF = ROWS // 2
NB = HALF // BLOCK
EXT = HALF + 2 * HALO
DEAD = EXT // BLOCK
PAN = 128
UNROLL = 8
HC = PAN // 2
QC = HC // 4


def kernel(idx, basis_ref, stiff_ref, out_ref,
           sv, ox, ya, yh, zu, zd, g, pt, zt, ap, az, acc, r1, s2, r2, tot, fin,
           lsem, hs, hr, fs, fr, ys, yr, zus, zur, zds, zdr, s1s, s1r, s2s, s2r, s3s, s3r):
    r = lax.axis_index("row")
    c = lax.axis_index("col")
    core, x, zh = r % 2, (r // 2) % 4, r // 8
    a, b = c // 4, c % 4

    load_own = pltpu.make_async_copy(basis_ref, ox.at[pl.ds(HALO, ROWS)], lsem.at[0])
    load_own.start()
    load_s = pltpu.make_async_copy(stiff_ref, sv, lsem.at[1])
    load_s.start()

    def yb(d):
        return (b + d) % 4

    def ycol(d):
        return a * 4 + yb(d)

    def zcol(z):
        return z * 4 + b

    up_row, down_row = (r + 1) % 16, (r + 15) % 16
    barrier = pltpu.get_barrier_semaphore()

    def greet(i, carry):
        row = (r + i) % 16

        @pl.when(i > 0)
        def _():
            pl.semaphore_signal(barrier, inc=1, device_id=(row, c), device_id_type=MESH)

        for d in (1, 2, 3):
            pl.semaphore_signal(barrier, inc=1, device_id=(row, ycol(d)), device_id_type=MESH)
            pl.semaphore_signal(barrier, inc=1, device_id=(row, zcol((a + d) % 4)), device_id_type=MESH)
        return carry

    lax.fori_loop(0, 16, greet, 0)
    pl.semaphore_wait(barrier, 16 * 7 - 1)

    def remote(src, dst, ss, rs, dev):
        return pltpu.make_async_remote_copy(src_ref=src, dst_ref=dst, send_sem=ss, recv_sem=rs,
                                            device_id=dev, device_id_type=MESH)

    halo_up = remote(basis_ref.at[pl.ds(ROWS - HALO, HALO)], ox.at[pl.ds(0, HALO)], hs.at[0], hr.at[0], (up_row, c))
    halo_down = remote(basis_ref.at[pl.ds(0, HALO)], ox.at[pl.ds(ROWS + HALO, HALO)], hs.at[1], hr.at[1], (down_row, c))
    own_lo = basis_ref.at[pl.ds(0, HALF)]
    own_hi = basis_ref.at[pl.ds(HALF, HALF)]
    nxt, prv = (r, ycol(1)), (r, ycol(3))
    y_lo_n = remote(own_lo, ya.at[1, pl.ds(HALO, HALF)], ys.at[0], yr.at[0], nxt)
    y_hi_n = remote(own_hi, yh.at[1], ys.at[1], yr.at[1], nxt)
    y_hi_p = remote(own_hi, yh.at[0], ys.at[2], yr.at[2], prv)
    y_lo_p = remote(own_lo, ya.at[0, pl.ds(HALO, HALF)], ys.at[3], yr.at[3], prv)
    PIECE = HALF // 2
    y_lo_f = [remote(ya.at[1, pl.ds(HALO + p * PIECE, PIECE)], ya.at[2, pl.ds(HALO + p * PIECE, PIECE)],
                     ys.at[4 + p], yr.at[4 + p], nxt) for p in range(2)]
    y_hi_f = [remote(yh.at[0, pl.ds(p * PIECE, PIECE)], yh.at[2, pl.ds(p * PIECE, PIECE)],
                     ys.at[6 + p], yr.at[6 + p], prv) for p in range(2)]

    zup = (r, zcol((a + 1) % 4))
    zdn = (r, zcol((a + 3) % 4))
    DN = HALF + HALO
    UP_CUT = ((0, HALF // 2), (HALF // 2, HALF // 2))
    DN_CUT = ((0, HALF // 2 + BLOCK), (HALF // 2 + BLOCK, HALF // 2 + BLOCK))
    zu_cp, zd_cp = [], []
    for d in range(3):
        for p in range(2):
            o, n = UP_CUT[p]
            src = basis_ref.at[pl.ds(o, n)] if d == 0 else zu.at[d - 1, pl.ds(o, n)]
            zu_cp.append(remote(src, zu.at[d, pl.ds(o, n)], zus.at[2 * d + p], zur.at[2 * d + p], zup))
            o, n = DN_CUT[p]
            src = basis_ref.at[pl.ds(HALF - HALO + o, n)] if d == 0 else zd.at[d - 1, pl.ds(o, n)]
            zd_cp.append(remote(src, zd.at[d, pl.ds(o, n)], zds.at[2 * d + p], zdr.at[2 * d + p], zdn))

    for p in range(2):
        @pl.when(a < 3)
        def _():
            zu_cp[p].start()

        @pl.when(a > 0)
        def _():
            zd_cp[p].start()

    halo_up.start()
    halo_down.start()
    y_lo_n.start()
    y_hi_p.start()
    y_hi_n.start()
    y_lo_p.start()

    g[DEAD] = jnp.zeros((BLOCK, 2 * PAN), BF)

    halo_up.wait_recv()
    halo_down.wait_recv()
    fan_lo = [remote(ox.at[pl.ds(0, HALO)], ya.at[s - 1, pl.ds(0, HALO)], fs.at[s - 1], fr.at[s - 1], (r, ycol(dy)))
              for s, dy in ((1, 3), (2, 1), (3, 2))]
    fan_hi = [remote(ox.at[pl.ds(HALO + ROWS, HALO)], zd.at[d - 1, pl.ds(DN, HALO)], fs.at[2 + d], fr.at[2 + d],
                     (r, zcol((a + 4 - d) % 4))) for d in (1, 2, 3)]
    for cp in fan_lo:
        cp.start()
    for d in (1, 2, 3):
        @pl.when(a >= d)
        def _():
            fan_hi[d - 1].start()

    def apply(h, outs, lo=0, hi=NB):
        n = len(outs) * PAN

        def step(i, carry):
            row = h * NB + i
            lhs = jnp.concatenate([sv[0, row], sv[1, row]], axis=0)
            picked = jnp.concatenate(
                [g[idx[s, row]][:, 0:n] for s in range(CAP)], axis=0)
            res = jnp.dot(lhs, picked, preferred_element_type=F32).astype(BF)
            at = pl.ds(pl.multiple_of(i * BLOCK, BLOCK), BLOCK)
            for p, (ref, k) in enumerate(outs):
                for q in range(2):
                    ref[k, at, q * PAN:(q + 1) * PAN] = res[q * BLOCK:(q + 1) * BLOCK, p * PAN:(p + 1) * PAN]
            return carry

        lax.fori_loop(lo, hi, step, 0, unroll=UNROLL)

    def put(rows, at, lane):
        n = rows.shape[0] // BLOCK
        g[at:at + n, :, lane:lane + PAN] = rows.reshape(n, BLOCK, PAN)

    def take_y(s, lane):
        put(ya[s - 1], 0, lane)
        put(yh[s - 1, 0:HALO], DEAD - 2, lane)

    def turn_y(s, lo=0, hi=HALF):
        pt[0, s * PAN:(s + 1) * PAN, lo:hi] = ya[s - 1, HALO + lo:HALO + hi, :].T
        pt[1, s * PAN:(s + 1) * PAN, lo:hi] = yh[s - 1, lo:hi].T

    def keep(z, lo, res, more=False):
        for s in range(res.shape[0] // PAN):
            for half in range(2):
                at = s * PAN + half * HC
                rows = slice((lo + s) * HC, (lo + s + 1) * HC)
                if more:
                    acc[z, half, rows, :] += res[at:at + HC, :]
                else:
                    acc[z, half, rows, :] = res[at:at + HC, :]

    def down(d, lo, hi, k0=0, k1=HALF):
        res = jnp.dot(pt[1, lo * PAN:hi * PAN, k0:k1], az[d, k0:k1, :], preferred_element_type=F32)
        if d == 0:
            res += jnp.dot(pt[0, lo * PAN:hi * PAN, k0:k1], ap[0, k0:k1, :], preferred_element_type=F32)
        keep(a + d, lo, res, k0 > 0)

    def up(d, s, k0=0, k1=HALF):
        keep(a - d, s, jnp.dot(zt[d - 1, :, k0:k1], ap[s, k0:k1, :], preferred_element_type=F32), k0 > 0)

    def pass_on(d):
        for p in range(2 * d, 2 * d + 2):
            @pl.when(a > d)
            def _():
                zu_cp[p].wait_recv()

            @pl.when((a > d) & (a < 3))
            def _():
                zu_cp[p + 2].start()

            @pl.when(a + d < 3)
            def _():
                zd_cp[p].wait_recv()

            @pl.when((a + d < 3) & (a > 0))
            def _():
                zd_cp[p + 2].start()

    load_own.wait()
    load_s.wait()
    put(ox[0:EXT, :], 0, 0)
    apply(0, [(ap, 0)])
    pt[0, 0:PAN, :] = ox[HALO:HALO + HALF, :].T
    pt[1, 0:PAN, :] = ox[HALO + HALF:HALO + ROWS, :].T

    pass_on(0)

    y_lo_n.wait_recv()
    y_hi_p.wait_recv()
    for p in range(2):
        y_lo_f[p].start()
        y_hi_f[p].start()

    put(ox[HALF:HALF + EXT, :], 0, 0)

    @pl.when(a < 3)
    def _():
        fan_hi[0].wait_recv()
        put(zd[0], 0, PAN)
        apply(1, [(az, 0), (az, 1)])

    @pl.when(a == 3)
    def _():
        apply(1, [(az, 0)])

    pass_on(1)
    y_hi_n.wait_recv()
    y_lo_p.wait_recv()
    for s in (1, 2):
        fan_lo[s - 1].wait_recv()
        turn_y(s)

    @pl.when(a > 0)
    def _():
        take_y(1, 0)
        take_y(2, PAN)
        apply(0, [(ap, 1), (ap, 2)])
        zt[0] = zu[0].T
        for s in (0, 1, 2):
            up(1, s)

    @pl.when(a > 1)
    def _():
        zt[1] = zu[1].T
        for s in (0, 1, 2):
            up(2, s)

    down(0, 0, 3)

    @pl.when(a < 3)
    def _():
        down(1, 0, 3)

    @pl.when(a < 2)
    def _():
        fan_hi[1].wait_recv()
        put(zd[1], 0, 0)
        apply(1, [(az, 2)])
        down(2, 0, 3)

    EARLY, LATE = (0, 3), (3, 4)

    def each(fn, which):
        def step(z, carry):
            far = (z - a == 3) | (a - z == 3)
            if which == "early":
                @pl.when(jnp.logical_not(far))
                def _():
                    fn(z, 0, *EARLY)
            elif which == "late":
                @pl.when(far)
                def _():
                    fn(z, 0, *EARLY)
                fn(z, 1, *LATE)
            else:
                fn(z, 0, *EARLY)
                fn(z, 1, *LATE)
            return carry
        lax.fori_loop(0, 4, step, 0)

    def pair_copy(z, w, lo, hi):
        rows = pl.ds(lo * HC, (hi - lo) * HC)
        return remote(acc.at[z, 1 - core, rows], r1.at[z, rows], s1s.at[z, w], s1r.at[z, w],
                      (zh * 8 + x * 2 + (1 - core), c))

    def x_copy(z, w, lo, hi, d):
        rows = pl.ds(lo * QC, (hi - lo) * QC)
        return remote(s2.at[z, d - 1, rows], r2.at[z, d - 1, rows], s2s.at[z, w, d - 1], s2r.at[z, w, d - 1],
                      (zh * 8 + ((x + d) % 4) * 2 + core, c))

    def owner(z, s):
        y = (b + s + (s // 2) * (1 - 2 * (s % 2))) % 4
        left = jnp.where(z < a, z * 4 + b, a * 4 + y)
        right = jnp.where(z < a, a * 4 + y, z * 4 + b)
        place = jnp.where(z < a, 0, 2) + zh
        return left, right, place, (z != a) | (y <= b)

    share = pl.ds(pl.multiple_of(core * HC + x * QC, QC), QC)

    def last_copy(z, s, left, right, place):
        return remote(tot.at[z, s], fin.at[place, share], s3s.at[z, s], s3r.at[place], (left, right))

    def pair_send(z, w, lo, hi):
        pair_copy(z, w, lo, hi).start()

    def pair_sum(z, w, lo, hi):
        pair_copy(z, w, lo, hi).wait_recv()
        for s in range(lo, hi):
            for d in (1, 2, 3):
                rows = pl.ds(pl.multiple_of(s * HC + ((x + d) % 4) * QC, QC), QC)
                s2[z, d - 1, s * QC:(s + 1) * QC, :] = (acc[z, core, rows, :] + r1[z, rows, :]).astype(BF)
        for d in (1, 2, 3):
            x_copy(z, w, lo, hi, d).start()

    def x_sum(z, w, lo, hi):
        for d in (1, 2, 3):
            x_copy(z, w, lo, hi, d).wait_recv()
        for s in range(lo, hi):
            rows = pl.ds(pl.multiple_of(s * HC + x * QC, QC), QC)
            part = acc[z, core, rows, :] + r1[z, rows, :]
            for d in (1, 2, 3):
                part += r2[z, d - 1, s * QC:(s + 1) * QC, :].astype(F32)
            left, right, place, used = owner(z, s)
            here = (left == r) & (right == c)

            @pl.when(used & here)
            def _():
                fin[place, share, :] = part

            @pl.when(used & jnp.logical_not(here))
            def _():
                tot[z, s] = part
                last_copy(z, s, left, right, place).start()

    each(pair_send, "early")
    each(pair_sum, "early")

    E0 = HALO + PIECE
    N0 = E0 // BLOCK - 4
    READY = DN_CUT[0][1] // BLOCK - 5
    for p in range(2):
        lo, hi = p * PIECE, (p + 1) * PIECE
        y_lo_f[p].wait_recv()
        y_hi_f[p].wait_recv()
        if p == 0:
            fan_lo[2].wait_recv()
        turn_y(3, lo, hi)

        @pl.when(a == 3)
        def _():
            zu_cp[4 + p].wait_recv()
            zt[2, :, lo:hi] = zu[2, lo:hi].T
            for s in (0, 1, 2):
                up(3, s, lo, hi)

        @pl.when(a == 0)
        def _():
            zd_cp[4 + p].wait_recv()
            o, n = DN_CUT[p]
            put(zd[2, o:o + n], o // BLOCK, 0)
            if p == 0:
                apply(1, [(az, 3)], 0, READY)
                down(3, 0, 3, 0, READY * BLOCK)
            else:
                fan_hi[2].wait_recv()
                put(zd[2, DN:EXT], DEAD - 2, 0)
                apply(1, [(az, 3)], READY, NB)
                down(3, 0, 3, READY * BLOCK, HALF)
                down(3, 3, 4)

        @pl.when(a > 0)
        def _():
            if p == 0:
                put(ya[2, 0:E0], 0, 0)
                apply(0, [(ap, 3)], 0, N0)
            else:
                put(ya[2, E0:HALO + HALF], E0 // BLOCK, 0)
                put(yh[2, 0:HALO], DEAD - 2, 0)
                apply(0, [(ap, 3)], N0, NB)

        for d in (1, 2, 3):
            @pl.when(a >= d)
            def _():
                if p == 0:
                    up(d, 3, 0, N0 * BLOCK)
                else:
                    up(d, 3, N0 * BLOCK, HALF)

        down(0, 3, 4, lo, hi)
        for d in (1, 2):
            @pl.when(a + d < 4)
            def _():
                down(d, 3, 4, lo, hi)

        if p == 0:
            each(x_sum, "early")

    each(pair_send, "late")
    each(pair_sum, "late")
    each(x_sum, "late")

    zi, yi = r // 4, r % 4
    cross = zi < a
    plane = (zi == a) & (yi <= b)

    def fin_wait(place, rows):
        part = fin.at[place, pl.ds(0, rows)]
        remote(part, part, s3s.at[0, 0], s3r.at[place], (r, other)).wait_recv()

    other = ycol(1)
    for place in range(4):
        if place < 2:
            wanted, here = cross, (yi == b) & (zh == place)
        else:
            wanted, here = cross | plane, plane & (zh == place - 2)

        @pl.when(wanted & here)
        def _():
            fin_wait(place, PAN - QC)

        @pl.when(wanted & jnp.logical_not(here))
        def _():
            fin_wait(place, PAN)

    @pl.when(cross)
    def _():
        out_ref[...] = (fin[0] + fin[1]) + (fin[2] + fin[3])

    @pl.when(plane)
    def _():
        out_ref[...] = fin[2] + fin[3]

    @pl.when(jnp.logical_not(cross | plane))
    def _():
        out_ref[...] = jnp.zeros_like(out_ref)

    for cp in [halo_up, halo_down, y_lo_n, y_hi_n, y_hi_p, y_lo_p] + y_lo_f + y_hi_f + fan_lo:
        cp.wait_send()
    for d in (1, 2, 3):
        @pl.when(a >= d)
        def _():
            fan_hi[d - 1].wait_send()

        @pl.when((a >= d - 1) & (a < 3))
        def _():
            zu_cp[2 * d - 2].wait_send()
            zu_cp[2 * d - 1].wait_send()

        @pl.when((a + d - 1 <= 3) & (a > 0))
        def _():
            zd_cp[2 * d - 2].wait_send()
            zd_cp[2 * d - 1].wait_send()

    def drain(z, w, lo, hi):
        pair_copy(z, w, lo, hi).wait_send()
        for d in (1, 2, 3):
            x_copy(z, w, lo, hi, d).wait_send()
        for s in range(lo, hi):
            left, right, place, used = owner(z, s)

            @pl.when(used & jnp.logical_not((left == r) & (right == c)))
            def _():
                last_copy(z, s, left, right, place).wait_send()

    each(drain, "all")


def shards(basis, stiffness, block_cols, block_counts):
    dma = pltpu.SemaphoreType.DMA
    rows = jnp.arange(2 * NB, dtype=jnp.int32)
    first = lax.axis_index("row") * (2 * NB) - 2 + (rows // NB) * NB
    live = jnp.arange(CAP, dtype=jnp.int32)[:, None] < block_counts[None, :]
    idx = jnp.where(live, block_cols.T - first[None, :], DEAD)
    out = pl.pallas_call(
        kernel,
        out_shape=jax.ShapeDtypeStruct((PAN, 2 * PAN), F32),
        in_specs=[
            pl.BlockSpec(memory_space=pltpu.SMEM),
            pl.BlockSpec(memory_space=pltpu.HBM),
            pl.BlockSpec(memory_space=pltpu.HBM),
        ],
        out_specs=pl.BlockSpec(memory_space=pltpu.VMEM),
        scratch_shapes=[
            pltpu.VMEM((2, 2 * NB, BLOCK, CAP * BLOCK), BF),
            pltpu.VMEM((ROWS + 2 * HALO, PAN), BF),
            pltpu.VMEM((3, HALO + HALF, PAN), BF),
            pltpu.VMEM((3, HALF, PAN), BF),
            pltpu.VMEM((3, HALF, PAN), BF),
            pltpu.VMEM((3, EXT, PAN), BF),
            pltpu.VMEM((DEAD + 1, BLOCK, 2 * PAN), BF),
            pltpu.VMEM((2, 4 * PAN, HALF), BF),
            pltpu.VMEM((3, PAN, HALF), BF),
            pltpu.VMEM((4, HALF, 2 * PAN), BF),
            pltpu.VMEM((4, HALF, 2 * PAN), BF),
            pltpu.VMEM((4, 2, 4 * HC, 2 * PAN), F32),
            pltpu.VMEM((4, 4 * HC, 2 * PAN), F32),
            pltpu.VMEM((4, 3, 4 * QC, 2 * PAN), BF),
            pltpu.VMEM((4, 3, 4 * QC, 2 * PAN), BF),
            pltpu.VMEM((4, 4, QC, 2 * PAN), F32),
            pltpu.VMEM((4, PAN, 2 * PAN), F32),
            dma((2,)), dma((2,)), dma((2,)), dma((6,)), dma((6,)), dma((8,)), dma((8,)),
            dma((6,)), dma((6,)), dma((6,)), dma((6,)),
            dma((4, 2)), dma((4, 2)), dma((4, 2, 3)), dma((4, 2, 3)), dma((4, 4)), dma((4,)),
        ],
        compiler_params=pltpu.CompilerParams(
            collective_id=0, has_side_effects=True, vmem_limit_bytes=56 * 2**20),
        cost_estimate=pl.CostEstimate(flops=8 * 10**9, bytes_accessed=10 * 2**20, transcendentals=0),
    )(idx, basis, stiffness)
    return out.reshape(PAN, 2, PAN)


def solution(mesh):
    return jax.shard_map(
        shards,
        mesh=mesh,
        in_specs=(P("row", "col"), P(None, "row", None, None), P("row", None), P("row")),
        out_specs=P("row", None, "col"),
        check_vma=False,
    )
```

time: 84.1 us -> 76.5 us (0.910); the launches traced: 82.5 us -> 76.4 us
  Pallas kernels: 79.4 us -> 73.5 us
    pallas_call x1, Pallas kernels: 79.4 us -> 73.5 us  [shards(): pl.pallas_call(kernel, out_shape=jax.ShapeDtypeStruct((PAN, 2 * PAN), F32...]
where the time goes in v2:
time: 76.5 us; the launch traced here: 76.4 us
  Pallas kernels  73.5 us (96%)
  local copies, waits for them, and re-layouts  1.62 us (2%)
  other arithmetic  1.29 us (2%)
    pallas_call x1, Pallas kernels, shards(): pl.pallas_call(kernel, out_shape=jax.ShapeDtypeStruct((PAN, 2 * PAN), F32...  73.5 us
    reshape x1, local copies, waits for them, and re-layouts, shards(): return out.reshape(PAN, 2, PAN)  1.62 us

profile of v2, /device:TPU:97, one launch (start us, length us, event | category | flops | bytes accessed | tf_op | source)
XLA Modules:
  0.0 76.4 jit_solution(17020066635098085816)
XLA Ops:
  0.0 1.3 %bitcast_select_fusion.idx = s32[8,64]{1,0:T(8,128)} fusion(s32[64,8]{0,1:T(8,128)} %param.6, s32[64]{0:T(128)S(1)} %fusion.1, s32[64]{0:T(128)} %param.7), kind=kLoop, calls=%fused_computation | loop fusion | flops 1536 | bytes 4608 | tf_op jit(solution)/shard_map/jit(_where)/select_n | solution.py:470
  1.3 73.5 %shard_map.46 = f32[128,256]{1,0:T(8,128)} custom-call(s32[8,64]{1,0:T(8,128)} %bitcast_select_fusion.idx, bf16[4096,128]{1,0:T(8,128)(2,1)} %basis_ref.1, bf16[2,64,64,512]{3,2,1,0:T(8,128)(2,1)} %stiff_ref.1), custom_call_target="tpu_custom_call" | custom-call | flops 8000000000 | bytes 10485760 | tf_op jit(solution)/shard_map/pallas_call | solution.py:471
  74.8 1.6 %reshape.19 = f32[128,2,128]{2,1,0:T(2,128)} reshape(f32[128,256]{1,0:T(8,128)} %shard_map.46) | data formatting | bytes 262144 | tf_op jit(solution)/shard_map/reshape | solution.py:506
  (1 shorter events, 0.0 us)

commit v3 on v2

--- a/solution.py
+++ b/solution.py
@@ -22,7 +22,7 @@
 QC = HC // 4
 
 
-def kernel(idx, basis_ref, stiff_ref, out_ref,
+def kernel(cols_ref, counts_ref, basis_ref, stiff_ref, out_ref,
            sv, ox, ya, yh, zu, zd, g, pt, zt, ap, az, acc, r1, s2, r2, tot, fin,
            lsem, hs, hr, fs, fr, ys, yr, zus, zur, zds, zdr, s1s, s1r, s2s, s2r, s3s, s3r):
     r = lax.axis_index("row")
@@ -133,8 +133,11 @@
         def step(i, carry):
             row = h * NB + i
             lhs = jnp.concatenate([sv[0, row], sv[1, row]], axis=0)
-            picked = jnp.concatenate(
-                [g[idx[s, row]][:, 0:n] for s in range(CAP)], axis=0)
+            first = r * (2 * NB) + h * NB - 2
+            picks = [i + 2] + [jnp.clip(cols_ref[s, row] - first, 0, DEAD) for s in range(1, CAP)]
+            for s in range(3, CAP):
+                picks[s] = jnp.where(s < counts_ref[row], picks[s], DEAD)
+            picked = jnp.concatenate([g[k][:, 0:n] for k in picks], axis=0)
             res = jnp.dot(lhs, picked, preferred_element_type=F32).astype(BF)
             at = pl.ds(pl.multiple_of(i * BLOCK, BLOCK), BLOCK)
             for p, (ref, k) in enumerate(outs):
@@ -220,6 +223,17 @@
     def _():
         apply(1, [(az, 0)])
 
+    down(0, 0, 1)
+
+    @pl.when(a < 3)
+    def _():
+        down(1, 0, 1)
+
+    @pl.when(a > 0)
+    def _():
+        zt[0] = zu[0].T
+        up(1, 0)
+
     pass_on(1)
     y_hi_n.wait_recv()
     y_lo_p.wait_recv()
@@ -232,8 +246,7 @@
         take_y(1, 0)
         take_y(2, PAN)
         apply(0, [(ap, 1), (ap, 2)])
-        zt[0] = zu[0].T
-        for s in (0, 1, 2):
+        for s in (1, 2):
             up(1, s)
 
     @pl.when(a > 1)
@@ -242,11 +255,11 @@
         for s in (0, 1, 2):
             up(2, s)
 
-    down(0, 0, 3)
+    down(0, 1, 3)
 
     @pl.when(a < 3)
     def _():
-        down(1, 0, 3)
+        down(1, 1, 3)
 
     @pl.when(a < 2)
     def _():
@@ -322,15 +335,14 @@
 
             @pl.when(used & here)
             def _():
-                fin[place, share, :] = part
+                fin[place, share, :] = part.astype(BF)
 
             @pl.when(used & jnp.logical_not(here))
             def _():
-                tot[z, s] = part
+                tot[z, s] = part.astype(BF)
                 last_copy(z, s, left, right, place).start()
 
     each(pair_send, "early")
-    each(pair_sum, "early")
 
     E0 = HALO + PIECE
     N0 = E0 // BLOCK - 4
@@ -390,9 +402,10 @@
                 down(d, 3, 4, lo, hi)
 
         if p == 0:
-            each(x_sum, "early")
+            each(pair_sum, "early")
 
     each(pair_send, "late")
+    each(x_sum, "early")
     each(pair_sum, "late")
     each(x_sum, "late")
 
@@ -421,11 +434,11 @@
 
     @pl.when(cross)
     def _():
-        out_ref[...] = (fin[0] + fin[1]) + (fin[2] + fin[3])
+        out_ref[...] = (fin[0].astype(F32) + fin[1].astype(F32)) + (fin[2].astype(F32) + fin[3].astype(F32))
 
     @pl.when(plane)
     def _():
-        out_ref[...] = fin[2] + fin[3]
+        out_ref[...] = fin[2].astype(F32) + fin[3].astype(F32)
 
     @pl.when(jnp.logical_not(cross | plane))
     def _():
@@ -464,14 +477,11 @@
 
 def shards(basis, stiffness, block_cols, block_counts):
     dma = pltpu.SemaphoreType.DMA
-    rows = jnp.arange(2 * NB, dtype=jnp.int32)
-    first = lax.axis_index("row") * (2 * NB) - 2 + (rows // NB) * NB
-    live = jnp.arange(CAP, dtype=jnp.int32)[:, None] < block_counts[None, :]
-    idx = jnp.where(live, block_cols.T - first[None, :], DEAD)
     out = pl.pallas_call(
         kernel,
         out_shape=jax.ShapeDtypeStruct((PAN, 2 * PAN), F32),
         in_specs=[
+            pl.BlockSpec(memory_space=pltpu.SMEM),
             pl.BlockSpec(memory_space=pltpu.SMEM),
             pl.BlockSpec(memory_space=pltpu.HBM),
             pl.BlockSpec(memory_space=pltpu.HBM),
@@ -493,8 +503,8 @@
             pltpu.VMEM((4, 4 * HC, 2 * PAN), F32),
             pltpu.VMEM((4, 3, 4 * QC, 2 * PAN), BF),
             pltpu.VMEM((4, 3, 4 * QC, 2 * PAN), BF),
-            pltpu.VMEM((4, 4, QC, 2 * PAN), F32),
-            pltpu.VMEM((4, PAN, 2 * PAN), F32),
+            pltpu.VMEM((4, 4, QC, 2 * PAN), BF),
+            pltpu.VMEM((4, PAN, 2 * PAN), BF),
             dma((2,)), dma((2,)), dma((2,)), dma((6,)), dma((6,)), dma((8,)), dma((8,)),
             dma((6,)), dma((6,)), dma((6,)), dma((6,)),
             dma((4, 2)), dma((4, 2)), dma((4, 2, 3)), dma((4, 2, 3)), dma((4, 4)), dma((4,)),
@@ -502,7 +512,7 @@
         compiler_params=pltpu.CompilerParams(
             collective_id=0, has_side_effects=True, vmem_limit_bytes=56 * 2**20),
         cost_estimate=pl.CostEstimate(flops=8 * 10**9, bytes_accessed=10 * 2**20, transcendentals=0),
-    )(idx, basis, stiffness)
+    )(block_cols.T, block_counts, basis, stiffness)
     return out.reshape(PAN, 2, PAN)
 
 

time: 76.5 us -> 69.4 us (0.907)
  Pallas kernels: 73.5 us -> 67.6 us
  other arithmetic: 1.29 us -> 0 us
    pallas_call x1, Pallas kernels: 73.5 us -> 67.6 us  [shards(): pl.pallas_call(kernel, out_shape=jax.ShapeDtypeStruct((PAN, 2 * PAN), F32...]
    select_n x1 -> x0, other arithmetic: 1.28 us -> none  [shards(): idx = jnp.where(live, block_cols.T - first[None, :], DEAD)]
where the time goes in v3:
time: 69.4 us; the launch traced here: 69.3 us
  Pallas kernels  67.6 us (97%)
  local copies, waits for them, and re-layouts  1.62 us (2%)
    pallas_call x1, Pallas kernels, shards(): pl.pallas_call(kernel, out_shape=jax.ShapeDtypeStruct((PAN, 2 * PAN), F32...  67.6 us
    reshape x1, local copies, waits for them, and re-layouts, shards(): return out.reshape(PAN, 2, PAN)  1.62 us

profile of v3, /device:TPU:97, one launch (start us, length us, event | category | flops | bytes accessed | tf_op | source)
XLA Modules:
  0.0 69.3 jit_solution(16722435832415094666)
XLA Ops:
  0.0 67.6 %shard_map.46 = f32[128,256]{1,0:T(8,128)} custom-call(s32[8,64]{1,0:T(8,128)} %bitcast.1, s32[64]{0:T(128)} %counts_ref.1, bf16[4096,128]{1,0:T(8,128)(2,1)} %basis_ref.1, bf16[2,64,64,512]{3,2,1,0:T(8,128)(2,1)} %stiff_ref.1), custom_call_target="tpu_custom_call" | custom-call | flops 8000000000 | bytes 10485760 | tf_op jit(solution)/shard_map/pallas_call | solution.py:480
  67.7 1.6 %reshape.3 = f32[128,2,128]{2,1,0:T(2,128)} reshape(f32[128,256]{1,0:T(8,128)} %shard_map.46) | data formatting | bytes 262144 | tf_op jit(solution)/shard_map/reshape | solution.py:516

commit v4 on v3

--- a/solution.py
+++ b/solution.py
@@ -96,6 +96,8 @@
             src = basis_ref.at[pl.ds(HALF - HALO + o, n)] if d == 0 else zd.at[d - 1, pl.ds(o, n)]
             zd_cp.append(remote(src, zd.at[d, pl.ds(o, n)], zds.at[2 * d + p], zdr.at[2 * d + p], zdn))
 
+    y_lo_n.start()
+    y_hi_p.start()
     for p in range(2):
         @pl.when(a < 3)
         def _():
@@ -107,8 +109,6 @@
 
     halo_up.start()
     halo_down.start()
-    y_lo_n.start()
-    y_hi_p.start()
     y_hi_n.start()
     y_lo_p.start()
 
@@ -205,34 +205,34 @@
 
     pass_on(0)
 
+    put(ox[HALF:HALF + EXT, :], 0, 0)
+
+    @pl.when(a < 3)
+    def _():
+        fan_hi[0].wait_recv()
+        put(zd[0], 0, PAN)
+        apply(1, [(az, 0), (az, 1)])
+
+    @pl.when(a == 3)
+    def _():
+        apply(1, [(az, 0)])
+
+    down(0, 0, 1)
+
+    @pl.when(a < 3)
+    def _():
+        down(1, 0, 1)
+
+    @pl.when(a > 0)
+    def _():
+        zt[0] = zu[0].T
+        up(1, 0)
+
     y_lo_n.wait_recv()
     y_hi_p.wait_recv()
     for p in range(2):
         y_lo_f[p].start()
         y_hi_f[p].start()
-
-    put(ox[HALF:HALF + EXT, :], 0, 0)
-
-    @pl.when(a < 3)
-    def _():
-        fan_hi[0].wait_recv()
-        put(zd[0], 0, PAN)
-        apply(1, [(az, 0), (az, 1)])
-
-    @pl.when(a == 3)
-    def _():
-        apply(1, [(az, 0)])
-
-    down(0, 0, 1)
-
-    @pl.when(a < 3)
-    def _():
-        down(1, 0, 1)
-
-    @pl.when(a > 0)
-    def _():
-        zt[0] = zu[0].T
-        up(1, 0)
 
     pass_on(1)
     y_hi_n.wait_recv()
@@ -355,6 +355,16 @@
             fan_lo[2].wait_recv()
         turn_y(3, lo, hi)
 
+        @pl.when(a > 0)
+        def _():
+            if p == 0:
+                put(ya[2, 0:E0], 0, 0)
+                apply(0, [(ap, 3)], 0, N0)
+            else:
+                put(ya[2, E0:HALO + HALF], E0 // BLOCK, 0)
+                put(yh[2, 0:HALO], DEAD - 2, 0)
+                apply(0, [(ap, 3)], N0, NB)
+
         @pl.when(a == 3)
         def _():
             zu_cp[4 + p].wait_recv()
@@ -377,16 +387,6 @@
                 down(3, 0, 3, READY * BLOCK, HALF)
                 down(3, 3, 4)
 
-        @pl.when(a > 0)
-        def _():
-            if p == 0:
-                put(ya[2, 0:E0], 0, 0)
-                apply(0, [(ap, 3)], 0, N0)
-            else:
-                put(ya[2, E0:HALO + HALF], E0 // BLOCK, 0)
-                put(yh[2, 0:HALO], DEAD - 2, 0)
-                apply(0, [(ap, 3)], N0, NB)
-
         for d in (1, 2, 3):
             @pl.when(a >= d)
             def _():
@@ -405,8 +405,8 @@
             each(pair_sum, "early")
 
     each(pair_send, "late")
+    each(pair_sum, "late")
     each(x_sum, "early")
-    each(pair_sum, "late")
     each(x_sum, "late")
 
     zi, yi = r // 4, r % 4

time: 69.4 us -> 68.9 us (level)
  no operation moved by 1% of the time
where the time goes in v4:
time: 68.9 us; the launch traced here: 68.8 us
  Pallas kernels  67.2 us (98%)
  local copies, waits for them, and re-layouts  1.62 us (2%)
    pallas_call x1, Pallas kernels, shards(): pl.pallas_call(kernel, out_shape=jax.ShapeDtypeStruct((PAN, 2 * PAN), F32...  67.2 us
    reshape x1, local copies, waits for them, and re-layouts, shards(): return out.reshape(PAN, 2, PAN)  1.62 us

profile of v4, /device:TPU:97, one launch (start us, length us, event | category | flops | bytes accessed | tf_op | source)
XLA Modules:
  0.0 68.8 jit_solution(14410940337334566226)
XLA Ops:
  0.0 67.2 %shard_map.46 = f32[128,256]{1,0:T(8,128)} custom-call(s32[8,64]{1,0:T(8,128)} %bitcast.1, s32[64]{0:T(128)} %counts_ref.1, bf16[4096,128]{1,0:T(8,128)(2,1)} %basis_ref.1, bf16[2,64,64,512]{3,2,1,0:T(8,128)(2,1)} %stiff_ref.1), custom_call_target="tpu_custom_call" | custom-call | flops 8000000000 | bytes 10485760 | tf_op jit(solution)/shard_map/pallas_call | solution.py:480
  67.2 1.6 %reshape.3 = f32[128,2,128]{2,1,0:T(2,128)} reshape(f32[128,256]{1,0:T(8,128)} %shard_map.46) | data formatting | bytes 262144 | tf_op jit(solution)/shard_map/reshape | solution.py:516
